TPU v7x, 32 devices: a whole 2x2x4 slice. The times are simulated.
32 devices in a mesh: seq: 8 (over y, x, core), head: 4 (over z).
Axes of the slice: x: 2, y: 2, z: 4, core: 2. Of those that a mesh axis runs over, the one named last changes fastest.
Arguments:
- queries: bfloat16 [128, 16384], P(None, 'head')
- cache_keys: bfloat16 [2, 32768, 1024], P(None, 'seq', 'head'), may hold values from -6 to 6
- cache_values: bfloat16 [2, 32768, 1024], P(None, 'seq', 'head'), may hold values from -6 to 6
- tree_keys: bfloat16 [128, 1024], P(None, 'head')
- tree_values: bfloat16 [128, 1024], P(None, 'head'), may hold values from -6 to 6
- ancestors: int32 [2, 64, 64], replicated, may hold values from 0 to 1, as said below
- filled_extents: int32 [2], replicated, may hold values from 1 to 32768, as said below
- out_weight: bfloat16 [16384, 16384], P('head', 'seq'), may hold values from -0.046875 to 0.046875
- residual: bfloat16 [128, 16384], P(None, 'seq'), may hold values from -6 to 6
- norm_gain: bfloat16 [16384], replicated, may hold values from 0.099609375 to 1.8984375
- vocab_weight: bfloat16 [16384, 65536], P(None, ('seq', 'head'))
- candidates: int32 [128], replicated, may hold values from 0 to 65535
- amateur: float32 [128], replicated, may hold values from -12 to -1
Outputs:
- hidden: bfloat16 [128, 16384], P(None, ('seq', 'head'))
- contrast: float32 [128], replicated
Inputs may be any that keep to these rules, and one draw needn't show every extreme that they name: Rows are nodes; node 0 is the root; every node's parent has a smaller index; ancestors[b, i, i] = 1. Positions 0 to filled_extents[b] - 1 of request b are live; some request has length 32768.
All inputs are finite; a program needn't handle non-finite values.
Results may differ from a plain program's by a relative error of at most 0.006.
Values may be sent and summed in bfloat16 or wider, within the bound.
A program may use at most 256 MiB of HBM per device.

v0:
```python
import jax
import jax.numpy as jnp
from jax import lax
from jax.sharding import PartitionSpec as P

NODES_REQ = 64
D = 16384
HD = 128


NEG_FILL = -1e30
EPSILON = 1e-05


def joined(x, axis, join):
    gathered = jax.tree.map(
        lambda a, kind: lax.all_gather(a.astype(kind), axis),
        x,
        (jnp.bfloat16, jnp.bfloat16, jnp.bfloat16),
    )

    def take(source):
        return jax.tree.map(
            lambda a, own: lax.dynamic_index_in_dim(a, source, 0, False).astype(own.dtype),
            gathered,
            x,
        )

    return lax.fori_loop(
        1, lax.axis_size(axis), lambda source, state: join(state, take(source)), take(0)
    )


def joined_2(part, axis, combine):
    gathered = jax.tree.map(lambda a: lax.all_gather(a, axis), part)

    def take(source):
        return jax.tree.map(lambda a: lax.dynamic_index_in_dim(a, source, 0, False), gathered)

    return lax.fori_loop(
        1, lax.axis_size(axis), lambda source, state: combine(state, take(source)), take(0)
    )


def blend(former, latter):
    highest = jnp.maximum(former[0], latter[0])
    factor_a = jnp.exp(former[0] - highest)
    factor_b = jnp.exp(latter[0] - highest)
    return (
        highest,
        former[1] * factor_a + latter[1] * factor_b,
        former[2] * factor_a[..., None] + latter[2] * factor_b[..., None],
    )


def join_vocab(former, latter):
    highest = jnp.maximum(former[0], latter[0])
    total = former[1] * jnp.exp(former[0] - highest) + latter[1] * jnp.exp(latter[0] - highest)
    return (highest, total, former[2] + latter[2])


def body(
    queries,
    cache_keys,
    cache_values,
    tree_keys,
    tree_values,
    ancestors,
    filled_extents,
    out_weight,
    residual,
    norm_gain,
    vocab_weight,
    candidates,
    amateur,
):
    requests, element_locations, kv_width = cache_keys.shape
    kv_local = kv_width // HD
    heads_local = queries.shape[1] // HD
    group_size = heads_local // kv_local
    score_scale = HD ** (-0.5)
    grouped = queries.reshape(requests, NODES_REQ, kv_local, group_size, HD)
    stored_lookup_entries = cache_keys.reshape(requests, element_locations, kv_local, HD)
    stored_content_entries = cache_values.reshape(requests, element_locations, kv_local, HD)
    insertion_start_index = lax.axis_index("seq") * element_locations
    entry_validity = (insertion_start_index + jnp.arange(element_locations, dtype=jnp.int32))[
        None, :
    ] < filled_extents[:, None]
    joint_visibility_filter = entry_validity[:, None, None, None, :]
    scores = (
        jnp.einsum(
            "bnkgd,bpkd->bkgnp", grouped, stored_lookup_entries, preferred_element_type=jnp.float32
        )
        * score_scale
    )
    scores = jnp.where(joint_visibility_filter, scores, NEG_FILL)
    local_max = scores.max(-1)
    guessed_branch_lookups = tree_keys.reshape(requests, NODES_REQ, kv_local, HD)
    guessed_branch_contents = tree_values.reshape(requests, NODES_REQ, kv_local, HD)
    tree_live = (ancestors > 0)[:, None, None, :, :]
    tree_scores = (
        jnp.einsum(
            "bnkgd,bjkd->bkgnj", grouped, guessed_branch_lookups, preferred_element_type=jnp.float32
        )
        * score_scale
    )
    tree_scores = jnp.where(tree_live, tree_scores, NEG_FILL)
    tree_max = tree_scores.max(-1)
    tree_weights = jnp.where(tree_live, jnp.exp(tree_scores - tree_max[..., None]), 0.0)
    tree_sum = tree_weights.sum(-1)
    tree_summed = jnp.einsum(
        "bkgnj,bjkd->bkgnd",
        tree_weights.astype(jnp.bfloat16),
        guessed_branch_contents,
        preferred_element_type=jnp.float32,
    )
    weights = jnp.where(joint_visibility_filter, jnp.exp(scores - local_max[..., None]), 0.0)
    weight_sum = weights.sum(-1)
    summed = jnp.einsum(
        "bkgnp,bpkd->bkgnd",
        weights.astype(jnp.bfloat16),
        stored_content_entries,
        preferred_element_type=jnp.float32,
    )
    highest, weight_sum, summed = joined((local_max, weight_sum, summed), "seq", blend)
    highest, weight_sum, summed = blend(
        (highest, weight_sum, summed), (tree_max, tree_sum, tree_summed)
    )
    attended = (
        (summed / weight_sum[..., None])
        .transpose(0, 3, 1, 2, 4)
        .reshape(requests * NODES_REQ, heads_local * HD)
        .astype(jnp.bfloat16)
    )
    projected = jnp.dot(attended, out_weight, preferred_element_type=jnp.float32)
    cols_seq = out_weight.shape[1]
    share_width = cols_seq // lax.axis_size("head")
    vocab_local = vocab_weight.shape[1]
    whole = lax.psum(projected.astype(jnp.bfloat16), "head").astype(jnp.float32)
    wide = (residual.astype(jnp.float32) + whole).astype(jnp.bfloat16)
    wide_f = wide.astype(jnp.float32)
    squares = lax.psum(jnp.sum(wide_f * wide_f, axis=1), "seq")
    gain_cols = lax.dynamic_slice_in_dim(norm_gain, lax.axis_index("seq") * cols_seq, cols_seq, 0)
    normed = (
        wide_f * lax.rsqrt(squares / D + EPSILON)[:, None] * gain_cols.astype(jnp.float32)
    ).astype(jnp.bfloat16)
    logits = jnp.dot(
        lax.all_gather(normed, "seq", axis=1, tiled=True),
        vocab_weight,
        preferred_element_type=jnp.float32,
    )
    hidden = lax.dynamic_slice_in_dim(wide, lax.axis_index("head") * share_width, share_width, 1)
    vocab_start = lax.axis_index(("seq", "head")) * vocab_local
    peak_logit = logits.max(axis=1)
    mass_sum = jnp.sum(jnp.exp(logits - peak_logit[:, None]), axis=1)
    matches = jnp.arange(vocab_local, dtype=jnp.int32)[None, :] + vocab_start == candidates[:, None]
    chosen = jnp.sum(jnp.where(matches, logits, 0.0), axis=1)
    peak_logit, mass_sum, chosen = joined_2(
        (peak_logit, mass_sum, chosen), ("seq", "head"), join_vocab
    )
    contrast = chosen - (peak_logit + jnp.log(mass_sum)) - amateur
    return (hidden, contrast)


def solution(mesh):
    in_specs = (
        P(None, "head"),
        P(None, "seq", "head"),
        P(None, "seq", "head"),
        P(None, "head"),
        P(None, "head"),
        P(),
        P(),
        P("head", "seq"),
        P(None, "seq"),
        P(),
        P(None, ("seq", "head")),
        P(),
        P(),
    )
    out_specs = (P(None, ("seq", "head")), P())
    return jax.shard_map(body, mesh=mesh, in_specs=in_specs, out_specs=out_specs, check_vma=False)
```

profile of v0, /device:TPU:0, one launch (start us, length us, event | category | flops | bytes accessed | tf_op | source)
XLA Modules:
  0.0 484.9 jit_solution(354190674399251556)
XLA Ops:
  7.2 1.4 copy.54
  8.7 6.9 %reshape.93 = bf16[2,4096,2,128]{3,2,1,0:T(2,128)(2,1)} reshape(bf16[2,4096,256]{2,1,0:T(8,128)(2,1)} %param.18) | data formatting | bytes 8388608 | tf_op jit(solution)/shard_map/reshape | solution.py:83
  15.6 6.9 %reshape.95 = bf16[2,4096,2,128]{3,2,1,0:T(2,128)(2,1)} reshape(bf16[2,4096,256]{2,1,0:T(8,128)(2,1)} %param.19) | data formatting | bytes 8388608 | tf_op jit(solution)/shard_map/reshape | solution.py:84
  22.6 26.8 %bitcast_reduce_fusion = (f32[2,2,16,64]{3,2,1,0:T(8,128)S(1)}, f32[2,2,4096,64,16]{2,3,4,1,0:T(8,128)}) fusion(pred[2,4096]{1,0:T(4,128)(4,1)S(1)} %broadcast_compare_fusion.1, bf16[2,64,2,16,128]{4,3,2,1,0:T(8,128)(2,1)S(1)} %bitcast.91, bf16[2,4096,2,128,1]{3,2,1,0,4:T(2,128)(2,1)} %bitcast.90), kind=kOutput, calls=%fused_computation.19 | convolution fusion | flops 4345294848 | bytes 72376320 | tf_op jit(solution)/shard_map/bnkgd,bpkd->bkgnp/dot_general | solution.py:91
  49.5 27.4 %fusion.22 = bf16[2,2,16,64,128]{4,3,2,1,0:T(8,128)(2,1)} fusion(bf16[2,4096,2,128,1]{3,2,1,0,4:T(2,128)(2,1)} %bitcast.94, f32[2,2,4096,64,16]{2,3,4,1,0:T(8,128)} %get-tuple-element.407, f32[2,2,16,64]{3,2,1,0:T(8,128)S(1)} %get-tuple-element.406, pred[2,4096]{1,0:T(4,128)(4,1)S(1)} %broadcast_compare_fusion.1), kind=kOutput, calls=%fused_computation.36 | convolution fusion | flops 4379377664 | bytes 72376320 | tf_op jit(solution)/shard_map/bkgnp,bpkd->bkgnd/dot_general | solution.py:119
  77.2 10.7 %all-gather = bf16[16,2,16,64]{3,2,1,0:T(8,128)(2,1)S(1)} all-gather(bf16[2,2,16,64]{3,2,1,0:T(8,128)(2,1)S(1)} %convert_element_type.123), channel_id=2, replica_groups=mesh['seq'=8,'head'=4] {'seq'}, dimensions={0}, use_global_device_ids=true | all-gather | bytes 73728 | tf_op jit(solution)/shard_map/all_gather | solution.py:17
  87.8 22.5 %fusion.13 = bf16[2,2,16,64]{3,2,1,0:T(8,128)(2,1)S(1)} fusion(f32[2,2,4096,64,16]{2,3,4,1,0:T(8,128)} %get-tuple-element.407, f32[2,2,16,64]{3,2,1,0:T(8,128)S(1)} %get-tuple-element.406, pred[2,4096]{1,0:T(4,128)(4,1)S(1)} %broadcast_compare_fusion.1), kind=kLoop, calls=%fused_computation.24 | loop fusion | flops 83881984 | bytes 67141632 | tf_op jit(solution)/shard_map/reduce_sum | solution.py:118
  110.4 9.5 %all-gather.1 = bf16[16,2,16,64]{3,2,1,0:T(8,128)(2,1)S(1)} all-gather(bf16[2,2,16,64]{3,2,1,0:T(8,128)(2,1)S(1)} %fusion.13), channel_id=3, replica_groups=mesh['seq'=8,'head'=4] {'seq'}, dimensions={0}, use_global_device_ids=true | all-gather | bytes 73728 | tf_op jit(solution)/shard_map/all_gather | solution.py:17
  119.9 1.1 fusion.21
  121.1 1.3 copy-done
  123.1 11.6 %all-gather.14.cloned.1.call-done = bf16[16,2,16,64,128]{4,3,2,1,0:T(8,128)(2,1)} async-done(((bf16[2,2,16,64,128]{4,3,2,1,0:T(8,128)(2,1)}), bf16[16,2,16,64,128]{4,3,2,1,0:T(8,128)(2,1)}) %all-gather.14.cloned.1.call-update) | async-done | bytes 8388624 | tf_op jit(solution)/shard_map/all_gather | solution.py:17
  134.7 1.5 slice_convert_fusion
  136.2 18.2 %while.38 = (s32[]{:T(128)}, f32[2,2,16,64]{3,2,1,0:T(8,128)S(1)}, f32[2,2,16,64]{3,2,1,0:T(8,128)S(1)}, f32[2,2,16,64,128]{4,3,2,1,0:T(8,128)S(1)}, bf16[8,2,2,...) while((s32[]{:T(128)}, f32[2,2,16,64]{3,2,1,0:T(8,128)S(1)}, ...), condition=%wide.region_3.4_spmd, body=%wide.region_2.3_spmd.sunk | while | flops 2129925 | bytes 5390487 | solution.py:29
  136.2 2.5 fusion.65
  138.8 2.5 fusion.65
  141.4 2.5 fusion.65
  144.0 2.5 fusion.65
  146.6 2.5 fusion.65
  149.2 2.5 fusion.65
  151.8 2.5 fusion.65
  154.4 3.6 fusion.29
  159.2 9.0 %convolution_convert_fusion = bf16[128,2048]{1,0:T(8,128)(2,1)} fusion(bf16[128,4096]{1,0:T(8,128)(2,1)S(1)} %convert_element_type.138, bf16[4096,2048]{1,0:T(8,128)(2,1)} %param.24), kind=kOutput, calls=%fused_computation.31 | convolution fusion | flops 2147745792 | bytes 18350080 | tf_op jit(solution)/shard_map/dot_general | solution.py:135
  168.9 37.7 %all-reduce.2.cloned.1.call-done = bf16[128,2048]{1,0:T(8,128)(2,1)} async-done(((bf16[128,2048]{1,0:T(8,128)(2,1)}), bf16[128,2048]{1,0:T(8,128)(2,1)}) %all-reduce.2.cloned.1.call-update) | async-done | bytes 524304 | tf_op jit(solution)/shard_map/psum | solution.py:139
  206.6 1.3 fusion.30
  208.0 12.9 %psum.15 = f32[128]{0:T(128)S(1)} all-reduce(f32[128]{0:T(128)S(1)} %get-tuple-element.400), channel_id=1, replica_groups=mesh['seq'=8,'head'=4] {'seq'}, use_global_device_ids=true, to_apply=%region_8.9 | all-reduce | flops 128 | bytes 1024 | tf_op jit(solution)/shard_map/psum | solution.py:142
  220.9 1.0 fusion.32
  222.6 34.2 %all-gather.12.cloned.1.call-done = bf16[128,16384]{1,0:T(8,128)(2,1)} async-done(((bf16[128,2048]{1,0:T(8,128)(2,1)}), bf16[128,16384]{1,0:T(8,128)(2,1)}) %all-gather.12.cloned.1.call-update) | async-done | bytes 4194320 | tf_op jit(solution)/shard_map/all_gather | solution.py:148
  256.8 24.0 %fusion.56 = (f32[128]{0:T(128)S(1)}, f32[128,2048]{1,0:T(8,128)S(1)}) fusion(bf16[128,16384]{1,0:T(8,128)(2,1)} %all-gather.12.cloned.1.call-done, bf16[16384,2048]{1,0:T(8,128)(2,1)} %param.27), kind=kOutput, calls=%fused_computation.83 | convolution fusion | flops 8590196736 | bytes 72352256 | tf_op jit(solution)/shard_map/dot_general | solution.py:147
  280.8 67.0 %all-gather.6 = f32[32,1,128]{2,1,0:T(1,128)S(1)} all-gather(f32[1,1,128]{2,1,0:T(1,128)S(1)} %bitcast.103), channel_id=5, replica_groups=mesh['seq'=8,'head'=4] {'seq','head'}, dimensions={0}, use_global_device_ids=true | all-gather | bytes 16896 | tf_op jit(solution)/shard_map/all_gather | solution.py:35
  348.2 63.0 %all-gather.7 = f32[32,1,128]{2,1,0:T(1,128)S(1)} all-gather(f32[1,1,128]{2,1,0:T(1,128)S(1)} %bitcast.105), channel_id=6, replica_groups=mesh['seq'=8,'head'=4] {'seq','head'}, dimensions={0}, use_global_device_ids=true | all-gather | bytes 16896 | tf_op jit(solution)/shard_map/all_gather | solution.py:35
  411.2 65.2 %all-gather.8 = f32[32,1,128]{2,1,0:T(1,128)S(1)} all-gather(f32[1,1,128]{2,1,0:T(1,128)S(1)} %bitcast.104), channel_id=7, replica_groups=mesh['seq'=8,'head'=4] {'seq','head'}, dimensions={0}, use_global_device_ids=true | all-gather | bytes 16896 | tf_op jit(solution)/shard_map/all_gather | solution.py:35
  476.4 1.4 while.39
  (81 shorter events, 5.8 us)
Async XLA Ops:
  7.2 127.5 %all-gather.14.cloned.1.call-start = ((), (), s32[]{:S(2)}) async-start(), calls=%async_computation.2 | async-start | bytes 9437184 | tf_op jit(solution)/shard_map/all_gather | solution.py:17
  15.6 6.9 %copy-start.5 = (s32[2]{0:T(128)S(1)}, s32[2]{0:T(128)}, u32[]{:S(2)}) copy-start(s32[2]{0:T(128)} %param.23) | copy-start | bytes 28
  49.5 27.5 %copy-start.2 = (s32[2,64,64]{2,1,0:T(8,128)S(1)}, s32[2,64,64]{2,1,0:T(8,128)}, u32[]{:S(2)}) copy-start(s32[2,64,64]{2,1,0:T(8,128)} %param.22) | copy-start | bytes 98308
  49.5 27.6 %copy-start.3 = (bf16[128,256]{1,0:T(8,128)(2,1)S(1)}, bf16[128,256]{1,0:T(8,128)(2,1)}, u32[]{:S(2)}) copy-start(bf16[128,256]{1,0:T(8,128)(2,1)} %param.20) | copy-start | bytes 196612
  49.5 27.7 %copy-start.4 = (bf16[128,256]{1,0:T(8,128)(2,1)S(1)}, bf16[128,256]{1,0:T(8,128)(2,1)}, u32[]{:S(2)}) copy-start(bf16[128,256]{1,0:T(8,128)(2,1)} %param.21) | copy-start | bytes 196612
  76.9 129.7 %all-reduce.2.cloned.1.call-start = ((), (), s32[]{:S(2)}) async-start(), calls=%async_computation | async-start | bytes 1048576 | tf_op jit(solution)/shard_map/psum | solution.py:139
  121.1 1.4 copy-start
  159.2 47.5 %copy-start.1 = (bf16[128,2048]{1,0:T(8,128)(2,1)S(1)}, bf16[128,2048]{1,0:T(8,128)(2,1)}, u32[]{:S(2)}) copy-start(bf16[128,2048]{1,0:T(8,128)(2,1)} %param.25) | copy-start | bytes 1572868
  168.2 88.6 %all-gather.12.cloned.1.call-start = ((), (), s32[]{:S(2)}) async-start(), calls=%async_computation.1 | async-start | bytes 4718592 | tf_op jit(solution)/shard_map/all_gather | solution.py:148
  222.6 125.2 %copy-start.6 = (s32[128]{0:T(128)S(1)}, s32[128]{0:T(128)}, u32[]{:S(2)}) copy-start(s32[128]{0:T(128)} %param.28) | copy-start | bytes 1540
  222.6 255.3 %copy-start.7 = (f32[128]{0:T(128)S(1)}, f32[128]{0:T(128)}, u32[]{:S(2)}) copy-start(f32[128]{0:T(128)} %param.29) | copy-start | bytes 1540
Sparse Core Ops, SparseCore 0:
  77.0 57.6 all-gather.13
  168.3 38.2 all-reduce.1
  222.0 34.7 all-gather.11
where the time goes:
time: 486 us; the launch traced here: 485 us
  blocking collectives  228 us (47%)
  matrix products  91.9 us (19%)
  waiting for transfers between devices  83.5 us (17%)
  other arithmetic  47.6 us (10%)
  local copies, waits for them, and re-layouts  18.7 us (4%)
  between operations  14 us (3%)
    all_gather x3, blocking collectives, joined_2(): gathered = jax.tree.map(lambda a: lax.all_gather(a, axis), part)  195 us
    psum x1, waiting for transfers between devices, body(): whole = lax.psum(projected.astype(jnp.bfloat16), 'head').astype(jnp.float32)  37.7 us
    all_gather x1, waiting for transfers between devices, body(): lax.all_gather(normed, 'seq', axis=1, tiled=True)  34.2 us
    dot_general x1, matrix products, body(): jnp.einsum('bkgnp,bpkd->bkgnd', weights.astype(jnp.bfloat16), stored_cont...  27.4 us
    dot_general x1, matrix products, body(): jnp.einsum('bnkgd,bpkd->bkgnp', grouped, stored_lookup_entries, preferred...  26.8 us
    dot_general x1, matrix products, body(): jnp.dot(lax.all_gather(normed, 'seq', axis=1, tiled=True), vocab_weight,...  24 us
    reduce_sum x1, other arithmetic, body(): weight_sum = weights.sum(-1)  22.5 us
    all_gather x2, blocking collectives, joined(): lax.all_gather(a.astype(kind), axis)  20.2 us
  transfers between devices with their start and end apart: 3, of which 3 were waited for; matrix products, arithmetic and copies ran while one was open for 5% of the time, Pallas kernels for 0%

commit v1 on v0

v1 whole, which is shorter than its diff:
```python
import functools
import math

import jax
import jax.numpy as jnp
from jax import lax
from jax.experimental import pallas as pl
from jax.experimental.pallas import tpu as pltpu
from jax.sharding import PartitionSpec as P

HD = 128
NEG_FILL = -1e30
EPSILON = 1e-05
MESH = pl.DeviceIdType.MESH
EXP2_SCALE = HD ** (-0.5) * math.log2(math.e)
LANES = 256


def attention_kernel(
    meta_ref, q_ref, k_ref, v_ref, tk_ref, tv_ref, tm_ref, acc_ref, st_ref, q_t, o_t, top, total
):
    b = pl.program_id(0)
    p = pl.program_id(2)
    block = k_ref.shape[1]
    rows = q_t.shape[1]

    @pl.when(p == 0)
    def _():
        for g in range(0, q_ref.shape[1], 2 * HD):
            pair = jnp.concatenate([q_ref[:, g : g + HD], q_ref[:, g + HD : g + 2 * HD]], axis=0)
            q_t[:, g // 2 : g // 2 + HD] = pair.astype(jnp.float32).T.astype(jnp.bfloat16)
        top[...] = jnp.full_like(top, NEG_FILL)
        total[...] = jnp.zeros_like(total)
        o_t[...] = jnp.zeros_like(o_t)

    def step(keys, values, live):
        values_t = values.T
        for c in range(0, rows, LANES):
            cols = slice(c, c + LANES)
            s = jnp.dot(keys, q_t[:, cols], preferred_element_type=jnp.float32)
            if live is not None:
                s = jnp.where(live(), s, NEG_FILL)
            before = top[:, cols]
            now = jnp.maximum(before, s.max(axis=0, keepdims=True) * EXP2_SCALE)
            w = jnp.exp2(s * EXP2_SCALE - now)
            factor = jnp.exp2(before - now)
            top[:, cols] = now
            total[:, cols] = total[:, cols] * factor + w.sum(axis=0, keepdims=True)
            o_t[:, cols] = o_t[:, cols] * factor + jnp.dot(
                values_t, w.astype(jnp.bfloat16), preferred_element_type=jnp.float32
            )

    left = meta_ref[b] - p * block

    @pl.when(left >= block)
    def _():
        step(k_ref[0], v_ref[0], None)

    @pl.when((left > 0) & (left < block))
    def _():
        step(
            k_ref[0],
            v_ref[0],
            lambda: lax.broadcasted_iota(jnp.int32, (block, LANES), 0) < left,
        )

    @pl.when(p == pl.num_programs(2) - 1)
    def _():
        @pl.when(meta_ref[pl.num_programs(0)] > 0)
        def _():
            step(tk_ref[...], tv_ref[...], lambda: tm_ref[0] > 0)

        width = acc_ref.shape[2]
        for i in range(acc_ref.shape[0]):
            cols = slice(i * width, (i + 1) * width)
            acc_ref[i] = o_t[:, cols].astype(jnp.bfloat16)
            row = lax.broadcasted_iota(jnp.int32, (8, width), 0)
            st_ref[i] = jnp.where(row == 0, top[:, cols], total[:, cols])


def attention(queries, keys, values, tree_keys, tree_values, ancestors, extents, seq):
    requests, positions, kv_width = keys.shape
    kv = kv_width // HD
    nodes = queries.shape[0] // requests
    group = queries.shape[1] // kv // HD
    rows = group * nodes
    pieces = seq // (requests * kv)
    width = rows // pieces
    block = min(1024, positions)
    me = lax.axis_index("seq")
    live = jnp.clip(extents - me * positions, 0, positions)
    meta = jnp.concatenate([live, (me == seq - 1).astype(jnp.int32)[None]])
    mask = jnp.tile(ancestors.transpose(0, 2, 1), (1, 1, LANES // nodes))
    cells = requests * kv * rows * positions
    return pl.pallas_call(
        attention_kernel,
        grid_spec=pltpu.PrefetchScalarGridSpec(
            num_scalar_prefetch=1,
            grid=(requests, kv, positions // block),
            in_specs=[
                pl.BlockSpec((nodes, group * HD), lambda b, g, p, m: (b, g)),
                pl.BlockSpec((1, block, HD), lambda b, g, p, m: (b, p, g)),
                pl.BlockSpec((1, block, HD), lambda b, g, p, m: (b, p, g)),
                pl.BlockSpec((nodes, HD), lambda b, g, p, m: (b, g)),
                pl.BlockSpec((nodes, HD), lambda b, g, p, m: (b, g)),
                pl.BlockSpec((1, nodes, LANES), lambda b, g, p, m: (b, 0, 0)),
            ],
            out_specs=[
                pl.BlockSpec((pieces, HD, width), lambda b, g, p, m: (b * kv + g, 0, 0)),
                pl.BlockSpec((pieces, 8, width), lambda b, g, p, m: (b * kv + g, 0, 0)),
            ],
            scratch_shapes=[
                pltpu.VMEM((HD, rows), jnp.bfloat16),
                pltpu.VMEM((HD, rows), jnp.float32),
                pltpu.VMEM((1, rows), jnp.float32),
                pltpu.VMEM((1, rows), jnp.float32),
            ],
        ),
        out_shape=[
            jax.ShapeDtypeStruct((seq, HD, width), jnp.bfloat16),
            jax.ShapeDtypeStruct((seq, 8, width), jnp.float32),
        ],
        compiler_params=pltpu.CompilerParams(vmem_limit_bytes=40 * 2**20),
        cost_estimate=pl.CostEstimate(
            flops=4 * HD * cells,
            bytes_accessed=4 * requests * positions * kv_width,
            transcendentals=cells,
        ),
    )(meta, queries, keys, values, tree_keys, tree_values, mask)


def toggled(index, flips, size):
    out = 0
    bit = 1
    while bit < size:
        out = out + ((index // bit + (flips // bit) % 2) % 2) * bit
        bit *= 2
    return out


def tail_kernel(
    seq, head, slots, nodes,
    acc_hbm, st_hbm, wo_hbm, res_ref, gain_ref, voc_hbm, cand_ref, amateur_ref,
    hid_ref, con_ref,
    racc, rst, att, wo, voc, psend, precv, hg, lacc, vst1, vst2,
    own_sem, wo_sem, voc_sem,
    acc_ss, acc_rs, st_ss, st_rs, att_ss, att_rs, p_ss, p_rs,
    z_ss, z_rs, c_ss, c_rs, t_ss, t_rs, v1_ss, v1_rs, v2_ss, v2_rs,
):
    s = lax.axis_index("seq")
    h = lax.axis_index("head")
    chips = seq // 2
    chip, core = s // 2, s % 2
    depth, share = wo.shape[1], wo.shape[2]
    cols = share * head
    vocab = voc_hbm.shape[1]
    width = racc.shape[2]
    pending = []

    def send(src, dst, ss, rs, to):
        copy = pltpu.make_async_remote_copy(
            src_ref=src, dst_ref=dst, send_sem=ss, recv_sem=rs, device_id=to, device_id_type=MESH
        )
        copy.start()
        pending.append(copy)
        return copy

    own_acc = pltpu.make_async_copy(acc_hbm.at[s], racc.at[0], own_sem.at[0])
    own_st = pltpu.make_async_copy(st_hbm.at[s], rst.at[0], own_sem.at[1])
    own_acc.start()
    own_st.start()

    def seq_peer(k):
        return (s + k) % seq

    def head_peer(k):
        return (h + k) % head

    barrier = pltpu.get_barrier_semaphore()
    for k in range(1, seq):
        pl.semaphore_signal(barrier, inc=1, device_id={"seq": seq_peer(k)}, device_id_type=MESH)
    for k in range(1, head):
        pl.semaphore_signal(barrier, inc=1, device_id={"head": head_peer(k)}, device_id_type=MESH)
    pl.semaphore_wait(barrier, seq + head - 2)

    acc_copies = []
    for k in range(1, seq):
        to = seq_peer(k)
        acc_copies.append(
            (
                send(st_hbm.at[to], rst.at[k], st_ss.at[k], st_rs.at[k], {"seq": to}),
                send(acc_hbm.at[to], racc.at[k], acc_ss.at[k], acc_rs.at[k], {"seq": to}),
            )
        )

    wo_copies = {}
    for k in list(range(1, head)) + [0]:
        start = pl.multiple_of(head_peer(k) * share, 128)
        wo_copies[k] = pltpu.make_async_copy(
            wo_hbm.at[:, pl.ds(start, share)], wo.at[k], wo_sem.at[k]
        )
        wo_copies[k].start()

    order = [(kc, e, i) for kc in range(chips) for e in range(2) for i in range(head // 2)]

    def voc_copies(t):
        kc, e, i = order[t]
        source = toggled(chip, kc, chips) * 2 + (core + e) % 2
        out = []
        for j in range(2):
            hs = (h + head - (2 * i + j)) % head
            row = pl.multiple_of(source * cols + hs * share, 128)
            out.append(
                pltpu.make_async_copy(
                    voc_hbm.at[pl.ds(row, share)],
                    voc.at[t % slots, pl.ds(j * share, share)],
                    voc_sem.at[t % slots, j],
                )
            )
        return out

    for t in range(min(slots, len(order))):
        for copy in voc_copies(t):
            copy.start()

    own_st.wait()
    own_acc.wait()
    for st, acc in acc_copies:
        st.wait_recv()
        acc.wait_recv()
    highest = rst[0, 0:1, :]
    for k in range(1, seq):
        highest = jnp.maximum(highest, rst[k, 0:1, :])
    number = jnp.zeros((HD, width), jnp.float32)
    weight = jnp.zeros((1, width), jnp.float32)
    for k in range(seq):
        factor = jnp.exp2(rst[k, 0:1, :] - highest)
        weight = weight + rst[k, 1:2, :] * factor
        number = number + racc[k].astype(jnp.float32) * factor
    mean = (number / weight).T
    row0 = pl.multiple_of((s // (seq // 2)) * nodes, nodes)
    wide = width // nodes * HD
    col0 = pl.multiple_of((s % (seq // 2)) * wide, 128)
    part = att.at[pl.ds(row0, nodes), pl.ds(col0, wide)]
    part[...] = jnp.concatenate(
        [mean[i : i + nodes] for i in range(0, width, nodes)], axis=1
    ).astype(jnp.bfloat16)
    att_copies = [
        send(part, part, att_ss.at[k], att_rs.at[k], {"seq": seq_peer(k)}) for k in range(1, seq)
    ]
    for copy in att_copies:
        copy.wait_recv()

    p_copies = []
    for k in list(range(1, head)) + [0]:
        wo_copies[k].wait()
        product = jnp.dot(att[...], wo[k], preferred_element_type=jnp.float32)
        if k:
            psend[k] = product.astype(jnp.bfloat16)
            p_copies.append(
                send(psend.at[k], precv.at[k], p_ss.at[k], p_rs.at[k], {"head": head_peer(k)})
            )
    for copy in p_copies:
        copy.wait_recv()
    for k in range(1, head):
        product = product + precv[k].astype(jnp.float32)
    mine = pl.ds(pl.multiple_of(h * share, 128), share)
    hidden = (res_ref[:, mine].astype(jnp.float32) + product).astype(jnp.bfloat16)
    hid_ref[...] = hidden
    hg[0, 0, 0] = hidden

    def spread(hr):
        piece = hg.at[0, 0, hr]
        out = {}
        for kc in range(1, chips):
            to = toggled(chip, kc, chips) * 2 + core
            out[kc] = send(
                piece, hg.at[kc, 0, hr], c_ss.at[kc, hr], c_rs.at[kc, hr], {"seq": to}
            )
        out[0] = to_partner(0, hr)
        return out

    def to_partner(kc, hr):
        return send(
            hg.at[kc, 0, hr],
            hg.at[kc, 1, hr],
            t_ss.at[kc, hr],
            t_rs.at[kc, hr],
            {"seq": chip * 2 + (core + 1) % 2},
        )

    z_copies = [
        send(hg.at[0, 0, 0], hg.at[0, 0, k], z_ss.at[k], z_rs.at[k], {"head": head_peer(k)})
        for k in range(1, head)
    ]
    spreads = [spread(0)]
    for hr in range(1, head):
        z_copies[hr - 1].wait_recv()
        spreads.append(spread(hr))
    partner = {0: [out[0] for out in spreads]}

    def forward(kc):
        partner[kc] = []
        for hr in range(head):
            spreads[hr][kc].wait_recv()
            partner[kc].append(to_partner(kc, hr))

    squares = jnp.zeros((hg.shape[3], 1), jnp.float32)
    lacc[...] = jnp.zeros_like(lacc)
    tile = min(512, vocab)
    done = 0
    for kc in range(chips):
        for e in range(2):
            if done + 1 < chips:
                forward(done + 1)
            done += 1
            if e == 1:
                for copy in partner[kc]:
                    copy.wait_recv()
            source = toggled(chip, kc, chips) * 2 + (core + e) % 2
            for i in range(head // 2):
                t = (kc * 2 + e) * (head // 2) + i
                parts = []
                for j in range(2):
                    hr = 2 * i + j
                    hs = (h + head - hr) % head
                    at = pl.multiple_of(source * cols + hs * share, 128)
                    x = hg[kc, e, hr].astype(jnp.float32)
                    squares = squares + jnp.sum(x * x, axis=1, keepdims=True)
                    gain = gain_ref[:, pl.ds(at, share)].astype(jnp.float32)
                    parts.append((x * gain).astype(jnp.bfloat16))
                x = jnp.concatenate(parts, axis=1)
                for copy in voc_copies(t):
                    copy.wait()

                @pl.loop(0, vocab // tile)
                def _(n):
                    span = pl.ds(pl.multiple_of(n * tile, 128), tile)
                    lacc[:, span] += jnp.dot(
                        x, voc[t % slots, :, span], preferred_element_type=jnp.float32
                    )

                if t + slots < len(order):
                    for copy in voc_copies(t + slots):
                        copy.start()

    logits = lacc[...] * lax.rsqrt(squares / (cols * seq) + EPSILON)
    peak = logits.max(axis=1, keepdims=True)
    mass = jnp.sum(jnp.exp(logits - peak), axis=1, keepdims=True)
    column = lax.broadcasted_iota(jnp.int32, logits.shape, 1) + (s * head + h) * vocab
    chosen = jnp.sum(jnp.where(column == cand_ref[...], logits, 0.0), axis=1, keepdims=True)
    lane = lax.broadcasted_iota(jnp.int32, (logits.shape[0], 128), 1)
    packed = jnp.where(lane == 0, peak, jnp.where(lane == 1, mass, chosen)).T
    vst1[0] = packed[0:8]

    def merged(ref, count):
        top = ref[0, 0:1, :]
        for k in range(1, count):
            top = jnp.maximum(top, ref[k, 0:1, :])
        total = jnp.zeros_like(top)
        picked = jnp.zeros_like(top)
        for k in range(count):
            total = total + ref[k, 1:2, :] * jnp.exp(ref[k, 0:1, :] - top)
            picked = picked + ref[k, 2:3, :]
        return top, total, picked

    copies = [
        send(vst1.at[0], vst1.at[k], v1_ss.at[k], v1_rs.at[k], {"seq": seq_peer(k)})
        for k in range(1, seq)
    ]
    for copy in copies:
        copy.wait_recv()
    top, total, picked = merged(vst1, seq)
    row = lax.broadcasted_iota(jnp.int32, (8, 128), 0)
    vst2[0] = jnp.where(row == 0, top, jnp.where(row == 1, total, picked))
    copies = [
        send(vst2.at[0], vst2.at[k], v2_ss.at[k], v2_rs.at[k], {"head": head_peer(k)})
        for k in range(1, head)
    ]
    for copy in copies:
        copy.wait_recv()
    top, total, picked = merged(vst2, head)
    con_ref[...] = picked - (top + jnp.log(total)) - amateur_ref[...]
    for copy in pending:
        copy.wait_send()


def tail(acc, stats, out_weight, residual, norm_gain, vocab_weight, candidates, amateur, head):
    seq, _, width = acc.shape
    depth, cols = out_weight.shape
    share = cols // head
    vocab = vocab_weight.shape[1]
    count = residual.shape[0]
    nodes = count // 2
    chips = seq // 2
    slots = min(7, seq * head // 2)
    dma = pltpu.SemaphoreType.DMA
    vmem = pl.BlockSpec(memory_space=pltpu.VMEM)
    hbm = pl.BlockSpec(memory_space=pl.ANY)
    bf16, f32 = jnp.bfloat16, jnp.float32
    hidden, contrast = pl.pallas_call(
        functools.partial(tail_kernel, seq, head, slots, nodes),
        in_specs=[hbm, hbm, hbm, vmem, vmem, hbm, vmem, vmem],
        out_specs=[vmem, vmem],
        out_shape=[
            jax.ShapeDtypeStruct((count, share), bf16),
            jax.ShapeDtypeStruct((1, count), f32),
        ],
        scratch_shapes=[
            pltpu.VMEM((seq, HD, width), bf16),
            pltpu.VMEM((seq, 8, width), f32),
            pltpu.VMEM((count, depth), bf16),
            pltpu.VMEM((head, depth, share), bf16),
            pltpu.VMEM((slots, 2 * share, vocab), bf16),
            pltpu.VMEM((head, count, share), bf16),
            pltpu.VMEM((head, count, share), bf16),
            pltpu.VMEM((chips, 2, head, count, share), bf16),
            pltpu.VMEM((count, vocab), f32),
            pltpu.VMEM((seq, 8, 128), f32),
            pltpu.VMEM((head, 8, 128), f32),
            dma((2,)), dma((head,)), dma((slots, 2)),
            dma((seq,)), dma((seq,)), dma((seq,)), dma((seq,)),
            dma((seq,)), dma((seq,)), dma((head,)), dma((head,)),
            dma((head,)), dma((head,)),
            dma((chips, head)), dma((chips, head)), dma((chips, head)), dma((chips, head)),
            dma((seq,)), dma((seq,)), dma((head,)), dma((head,)),
        ],
        compiler_params=pltpu.CompilerParams(
            collective_id=0, has_side_effects=True, vmem_limit_bytes=60 * 2**20
        ),
        cost_estimate=pl.CostEstimate(
            flops=2 * count * (depth * cols + vocab_weight.size),
            bytes_accessed=2 * (out_weight.size + vocab_weight.size),
            transcendentals=count * vocab,
        ),
    )(
        acc, stats, out_weight, residual, norm_gain[None, :], vocab_weight,
        candidates[:, None], amateur[None, :],
    )
    return hidden, contrast[0]


def solution(mesh):
    seq, head = mesh.shape["seq"], mesh.shape["head"]

    def body(
        queries, cache_keys, cache_values, tree_keys, tree_values, ancestors, filled_extents,
        out_weight, residual, norm_gain, vocab_weight, candidates, amateur,
    ):
        acc, stats = attention(
            queries, cache_keys, cache_values, tree_keys, tree_values, ancestors,
            filled_extents, seq,
        )
        return tail(
            acc, stats, out_weight, residual, norm_gain, vocab_weight, candidates, amateur, head
        )

    in_specs = (
        P(None, "head"),
        P(None, "seq", "head"),
        P(None, "seq", "head"),
        P(None, "head"),
        P(None, "head"),
        P(),
        P(),
        P("head", "seq"),
        P(None, "seq"),
        P(),
        P(None, ("seq", "head")),
        P(),
        P(),
    )
    out_specs = (P(None, ("seq", "head")), P())
    return jax.shard_map(body, mesh=mesh, in_specs=in_specs, out_specs=out_specs, check_vma=False)
```

time: 486 us -> 177 us (0.36)
  blocking collectives: 228 us -> 0 us
  Pallas kernels: 0 us -> 159 us
  matrix products: 91.9 us -> 0 us
  waiting for transfers between devices: 83.5 us -> 0 us
  other arithmetic: 47.6 us -> 0.74 us
  between operations: 14 us -> 0.68 us
    all_gather x5 -> x0, blocking collectives: 215 us -> none  [the longest x3 195 us: joined_2(): gathered = jax.tree.map(lambda a: lax.all_gather(a, axis), part)]
    pallas_call x0 -> x2, Pallas kernels: none -> 159 us  [the longest x1 106 us: tail(): pl.pallas_call(functools.partial(tail_kernel, seq, head, slots, nodes), i...]
    dot_general x6 -> x0, matrix products: 91.9 us -> none  [the longest x1 27.4 us: body(): jnp.einsum('bkgnp,bpkd->bkgnd', weights.astype(jnp.bfloat16), stored_cont...]
    all_gather x2 -> x0, waiting for transfers between devices: 45.7 us -> none  [the longest x1 34.2 us: body(): lax.all_gather(normed, 'seq', axis=1, tiled=True)]
    psum x1 -> x0, waiting for transfers between devices: 37.7 us -> none  [body(): whole = lax.psum(projected.astype(jnp.bfloat16), 'head').astype(jnp.float32)]
    reduce_sum x4 -> x0, other arithmetic: 24.9 us -> none  [the longest x1 22.5 us: body(): weight_sum = weights.sum(-1)]
    add x48 -> x0, other arithmetic: 18.9 us -> none  [the longest x7 17.7 us: blend(): former[2] * factor_a[..., None] + latter[2] * factor_b[..., None]]
    reshape x4 -> x0, local copies, waits for them, and re-layouts: 13.9 us -> none  [the longest x1 6.93 us: body(): cache_keys.reshape(requests, element_locations, kv_local, HD)]
  transfers between devices with their start and end apart: 3 -> 0, of which waited for: 3 -> 0; matrix products, arithmetic and copies ran while one was open for 5% -> 0% of each run, Pallas kernels for 0% -> 0%
where the time goes in v1:
time: 177 us; the launch traced here: 176 us
  Pallas kernels  159 us (90%)
  local copies, waits for them, and re-layouts  15.6 us (9%)
    pallas_call x1, Pallas kernels, tail(): pl.pallas_call(functools.partial(tail_kernel, seq, head, slots, nodes), i...  106 us
    pallas_call x1, Pallas kernels, attention(): pl.pallas_call(attention_kernel, grid_spec=pltpu.PrefetchScalarGridSpec(n...  53.1 us
    unnamed x16, local copies, waits for them, and re-layouts  11.6 us

profile of v1, /device:TPU:0, one launch (start us, length us, event | category | flops | bytes accessed | tf_op | source)
XLA Modules:
  0.0 175.7 jit_solution(2581554439976934210)
XLA Ops:
  0.6 0.7 subtract_clamp_fusion
  1.3 0.1 pad_add_fusion.meta_ref
  1.4 0.9 copy.15
  2.3 1.4 broadcast_in_dim.17.gain_ref
  3.7 1.4 copy.16.cand_ref
  5.1 0.2 tile.10.tm_ref
  5.4 0.0 copy-start.2
  5.4 2.2 %copy-done.2 = bf16[2,4096,256]{2,1,0:T(8,128)(2,1)S(1)} copy-done((bf16[2,4096,256]{2,1,0:T(8,128)(2,1)S(1)}, bf16[2,4096,256]{2,1,0:T(8,128)(2,1)}, u32[]{:S(2)}) %copy-start.2) | copy-done | bytes 4194328
  7.5 0.0 copy-start.3
  7.5 2.2 %copy-done.3 = bf16[2,4096,256]{2,1,0:T(8,128)(2,1)S(1)} copy-done((bf16[2,4096,256]{2,1,0:T(8,128)(2,1)S(1)}, bf16[2,4096,256]{2,1,0:T(8,128)(2,1)}, u32[]{:S(2)}) %copy-start.3) | copy-done | bytes 4194328
  9.7 0.0 copy-start.4
  9.7 1.2 copy-done.4
  11.0 0.0 copy-start.5
  11.0 0.8 copy-done.5
  11.8 0.0 copy-start.6
  11.8 0.8 copy-done.6
  12.6 53.1 %shard_map.140 = (bf16[8,128,512]{2,1,0:T(8,128)(2,1)S(1)}, f32[8,8,512]{2,1,0:T(8,128)S(1)}) custom-call(s32[3]{0:T(128)S(1)} %pad_add_fusion.meta_ref, bf16[128,4096]{1,0:T(8,128)(2,1)S(1)} %copy-done.4, bf16[2,4096,256]{2,1,0:T(8,128)(2,1)S(1)} %copy-done.2, bf16[2,4096,256]{2,1,0:T(8,128)(2,1)S(1)} %copy-done.3, bf16[128,256]{1,0:T(8,128)(2,1)S(1)} %copy-done.5, ...), custom_call_target="tpu_custom_call" | custom-call | flops 8589934592 | bytes 8388608 | tf_op jit(solution)/shard_map/pallas_call | solution.py:95
  65.8 0.0 copy-start
  65.8 1.0 copy-done
  66.7 0.0 copy-start.1
  66.7 0.7 copy-done.1
  67.4 105.6 %shard_map.141 = (bf16[128,512]{1,0:T(8,128)(2,1)}, f32[1,128]{1,0:T(1,128)}) custom-call(bf16[8,128,512]{2,1,0:T(8,128)(2,1)} %copy-done, f32[8,8,512]{2,1,0:T(8,128)} %copy-done.1, bf16[4096,2048]{1,0:T(8,128)(2,1)} %wo_hbm.1, bf16[128,2048]{1,0:T(8,128)(2,1)} %res_ref.1, bf16[1,16384]{1,0:T(2,128)(2,1)} %broadcast_in_dim.17.gain_ref, ...), custom_call_target="tpu_custom_call" | custom-call | flops 10737418240 | bytes 83886080 | tf_op jit(solution)/shard_map/pallas_call | solution.py:401
  173.0 1.6 copy.19
  174.5 1.2 copy.20
  (1 shorter events, 0.0 us)
Async XLA Ops:
  5.4 2.2 %copy-start.2 = (bf16[2,4096,256]{2,1,0:T(8,128)(2,1)S(1)}, bf16[2,4096,256]{2,1,0:T(8,128)(2,1)}, u32[]{:S(2)}) copy-start(bf16[2,4096,256]{2,1,0:T(8,128)(2,1)} %k_ref.1) | copy-start | bytes 12582916
  7.5 2.2 %copy-start.3 = (bf16[2,4096,256]{2,1,0:T(8,128)(2,1)S(1)}, bf16[2,4096,256]{2,1,0:T(8,128)(2,1)}, u32[]{:S(2)}) copy-start(bf16[2,4096,256]{2,1,0:T(8,128)(2,1)} %v_ref.1) | copy-start | bytes 12582916
  9.7 1.2 copy-start.4
  11.0 0.8 copy-start.5
  11.8 0.8 copy-start.6
  65.8 1.0 copy-start
  66.7 0.7 copy-start.1

commit v2 on v1

--- a/solution.py
+++ b/solution.py
@@ -14,10 +14,12 @@
 MESH = pl.DeviceIdType.MESH
 EXP2_SCALE = HD ** (-0.5) * math.log2(math.e)
 LANES = 256
+SUM_ROWS = 16
+WEIGHT_TYPE = jnp.bfloat16
 
 
 def attention_kernel(
-    meta_ref, q_ref, k_ref, v_ref, tk_ref, tv_ref, tm_ref, acc_ref, st_ref, q_t, o_t, top, total
+    meta_ref, q_ref, k_ref, v_ref, tk_ref, tv_ref, tm_ref, acc_ref, st_ref, q_t, o_t, top
 ):
     b = pl.program_id(0)
     p = pl.program_id(2)
@@ -30,25 +32,37 @@
             pair = jnp.concatenate([q_ref[:, g : g + HD], q_ref[:, g + HD : g + 2 * HD]], axis=0)
             q_t[:, g // 2 : g // 2 + HD] = pair.astype(jnp.float32).T.astype(jnp.bfloat16)
         top[...] = jnp.full_like(top, NEG_FILL)
-        total[...] = jnp.zeros_like(total)
         o_t[...] = jnp.zeros_like(o_t)
 
     def step(keys, values, live):
-        values_t = values.T
-        for c in range(0, rows, LANES):
-            cols = slice(c, c + LANES)
-            s = jnp.dot(keys, q_t[:, cols], preferred_element_type=jnp.float32)
+        values_t = jnp.concatenate(
+            [values.T, jnp.ones((SUM_ROWS, values.shape[0]), jnp.bfloat16)], axis=0
+        )
+
+        def scored(c):
+            s = jnp.dot(keys, q_t[:, c : c + LANES], preferred_element_type=jnp.float32)
             if live is not None:
                 s = jnp.where(live(), s, NEG_FILL)
-            before = top[:, cols]
-            now = jnp.maximum(before, s.max(axis=0, keepdims=True) * EXP2_SCALE)
-            w = jnp.exp2(s * EXP2_SCALE - now)
-            factor = jnp.exp2(before - now)
-            top[:, cols] = now
-            total[:, cols] = total[:, cols] * factor + w.sum(axis=0, keepdims=True)
-            o_t[:, cols] = o_t[:, cols] * factor + jnp.dot(
-                values_t, w.astype(jnp.bfloat16), preferred_element_type=jnp.float32
-            )
+            return s
+
+        ahead = scored(0)
+        late = None
+        for c in range(0, rows + LANES, LANES):
+            s = ahead
+            if c + LANES < rows:
+                ahead = scored(c + LANES)
+            if late is not None:
+                cols, factor, w = late
+                o_t[:, cols] = o_t[:, cols] * factor + jnp.dot(
+                    values_t, w, preferred_element_type=jnp.float32
+                )
+            if c < rows:
+                cols = slice(c, c + LANES)
+                before = top[:, cols]
+                now = jnp.maximum(before, s.max(axis=0, keepdims=True) * EXP2_SCALE)
+                w = jnp.exp2((s * EXP2_SCALE - now).astype(WEIGHT_TYPE)).astype(jnp.bfloat16)
+                top[:, cols] = now
+                late = (cols, jnp.exp2(before - now), w)
 
     left = meta_ref[b] - p * block
 
@@ -73,9 +87,9 @@
         width = acc_ref.shape[2]
         for i in range(acc_ref.shape[0]):
             cols = slice(i * width, (i + 1) * width)
-            acc_ref[i] = o_t[:, cols].astype(jnp.bfloat16)
+            acc_ref[i] = o_t[:HD, cols].astype(jnp.bfloat16)
             row = lax.broadcasted_iota(jnp.int32, (8, width), 0)
-            st_ref[i] = jnp.where(row == 0, top[:, cols], total[:, cols])
+            st_ref[i] = jnp.where(row == 0, top[:, cols], o_t[HD : HD + 1, cols])
 
 
 def attention(queries, keys, values, tree_keys, tree_values, ancestors, extents, seq):
@@ -111,8 +125,7 @@
             ],
             scratch_shapes=[
                 pltpu.VMEM((HD, rows), jnp.bfloat16),
-                pltpu.VMEM((HD, rows), jnp.float32),
-                pltpu.VMEM((1, rows), jnp.float32),
+                pltpu.VMEM((HD + SUM_ROWS, rows), jnp.float32),
                 pltpu.VMEM((1, rows), jnp.float32),
             ],
         ),
@@ -120,7 +133,7 @@
             jax.ShapeDtypeStruct((seq, HD, width), jnp.bfloat16),
             jax.ShapeDtypeStruct((seq, 8, width), jnp.float32),
         ],
-        compiler_params=pltpu.CompilerParams(vmem_limit_bytes=40 * 2**20),
+        compiler_params=pltpu.CompilerParams(vmem_limit_bytes=60 * 2**20),
         cost_estimate=pl.CostEstimate(
             flops=4 * HD * cells,
             bytes_accessed=4 * requests * positions * kv_width,
@@ -201,7 +214,8 @@
         )
         wo_copies[k].start()
 
-    order = [(kc, e, i) for kc in range(chips) for e in range(2) for i in range(head // 2)]
+    steps = sorted(range(chips), key=lambda kc: (kc.bit_count(), kc))
+    order = [(kc, e, i) for kc in steps for e in range(2) for i in range(head // 2)]
 
     def voc_copies(t):
         kc, e, i = order[t]
@@ -245,10 +259,29 @@
     part[...] = jnp.concatenate(
         [mean[i : i + nodes] for i in range(0, width, nodes)], axis=1
     ).astype(jnp.bfloat16)
+    def att_part(source):
+        row = pl.multiple_of((source // (seq // 2)) * nodes, nodes)
+        col = pl.multiple_of((source % (seq // 2)) * wide, 128)
+        return att.at[pl.ds(row, nodes), pl.ds(col, wide)]
+
+    def att_send(source, k, to):
+        piece = att_part(source)
+        return send(piece, piece, att_ss.at[k], att_rs.at[k], {"seq": to})
+
+    other = chip * 2 + (core + 1) % 2
     att_copies = [
-        send(part, part, att_ss.at[k], att_rs.at[k], {"seq": seq_peer(k)}) for k in range(1, seq)
+        att_send(s, 2 * kc, toggled(chip, kc, chips) * 2 + core) for kc in range(1, chips)
     ]
-    for copy in att_copies:
+    att_swaps = [att_send(s, 1, other)]
+    for kc in range(1, chips):
+        source = toggled(chip, kc, chips) * 2 + core
+        arrived = att_part(source)
+        pltpu.make_async_remote_copy(
+            src_ref=arrived, dst_ref=arrived, send_sem=att_ss.at[2 * kc],
+            recv_sem=att_rs.at[2 * kc], device_id={"seq": source}, device_id_type=MESH,
+        ).wait_recv()
+        att_swaps.append(att_send(source, 2 * kc + 1, other))
+    for copy in att_swaps:
         copy.wait_recv()
 
     p_copies = []
@@ -269,57 +302,68 @@
     hid_ref[...] = hidden
     hg[0, 0, 0] = hidden
 
-    def spread(hr):
-        piece = hg.at[0, 0, hr]
-        out = {}
-        for kc in range(1, chips):
-            to = toggled(chip, kc, chips) * 2 + core
-            out[kc] = send(
-                piece, hg.at[kc, 0, hr], c_ss.at[kc, hr], c_rs.at[kc, hr], {"seq": to}
-            )
-        out[0] = to_partner(0, hr)
-        return out
-
-    def to_partner(kc, hr):
-        return send(
-            hg.at[kc, 0, hr],
-            hg.at[kc, 1, hr],
-            t_ss.at[kc, hr],
-            t_rs.at[kc, hr],
-            {"seq": chip * 2 + (core + 1) % 2},
-        )
+    bits = [1 << i for i in range(chips.bit_length() - 1)]
+    near = {}
+    partner = {}
+
+    def parent(kc, hr):
+        held = [bit for bit in bits if kc & bit]
+        return kc ^ (held[0] if hr % 2 == 0 else held[-1])
+
+    def spread(kc, hr):
+        piece = hg.at[kc, 0, hr]
+        for bit in bits:
+            child = kc ^ bit
+            if child > kc and parent(child, hr) == kc:
+                near[child, hr] = send(
+                    piece,
+                    hg.at[child, 0, hr],
+                    c_ss.at[child, hr],
+                    c_rs.at[child, hr],
+                    {"seq": toggled(chip, bit, chips) * 2 + core},
+                )
+        partner[kc, hr] = send(
+            piece, hg.at[kc, 1, hr], t_ss.at[kc, hr], t_rs.at[kc, hr], {"seq": other}
+        )
+
+    def relay(kc, hr):
+        near[kc, hr].wait_recv()
+        spread(kc, hr)
 
     z_copies = [
         send(hg.at[0, 0, 0], hg.at[0, 0, k], z_ss.at[k], z_rs.at[k], {"head": head_peer(k)})
         for k in range(1, head)
     ]
-    spreads = [spread(0)]
+    spread(0, 0)
     for hr in range(1, head):
         z_copies[hr - 1].wait_recv()
-        spreads.append(spread(hr))
-    partner = {0: [out[0] for out in spreads]}
-
-    def forward(kc):
-        partner[kc] = []
-        for hr in range(head):
-            spreads[hr][kc].wait_recv()
-            partner[kc].append(to_partner(kc, hr))
+        spread(0, hr)
+        for bit in bits:
+            relay(bit, hr - 1)
+    late = sorted(kc for kc in range(1, chips) if kc not in bits)
 
     squares = jnp.zeros((hg.shape[3], 1), jnp.float32)
     lacc[...] = jnp.zeros_like(lacc)
     tile = min(512, vocab)
-    done = 0
-    for kc in range(chips):
+    rank = 0
+    for kc in steps:
         for e in range(2):
-            if done + 1 < chips:
-                forward(done + 1)
-            done += 1
+            if rank == 1:
+                for bit in bits:
+                    relay(bit, head - 1)
+            if rank >= 2:
+                for _ in range(-(-len(late) // (len(bits) * 2))):
+                    if late:
+                        done = late.pop(0)
+                        for hr in range(head):
+                            relay(done, hr)
+            rank += 1
             if e == 1:
-                for copy in partner[kc]:
-                    copy.wait_recv()
+                for hr in range(head):
+                    partner[kc, hr].wait_recv()
             source = toggled(chip, kc, chips) * 2 + (core + e) % 2
             for i in range(head // 2):
-                t = (kc * 2 + e) * (head // 2) + i
+                t = order.index((kc, e, i))
                 parts = []
                 for j in range(2):
                     hr = 2 * i + j
@@ -347,8 +391,11 @@
     logits = lacc[...] * lax.rsqrt(squares / (cols * seq) + EPSILON)
     peak = logits.max(axis=1, keepdims=True)
     mass = jnp.sum(jnp.exp(logits - peak), axis=1, keepdims=True)
+    count = logits.shape[0]
+    cand = jnp.broadcast_to(cand_ref[...].astype(jnp.float32), (count, count)).T
+    cand = cand[:, 0:1].astype(jnp.int32)
     column = lax.broadcasted_iota(jnp.int32, logits.shape, 1) + (s * head + h) * vocab
-    chosen = jnp.sum(jnp.where(column == cand_ref[...], logits, 0.0), axis=1, keepdims=True)
+    chosen = jnp.sum(jnp.where(column == cand, logits, 0.0), axis=1, keepdims=True)
     lane = lax.broadcasted_iota(jnp.int32, (logits.shape[0], 128), 1)
     packed = jnp.where(lane == 0, peak, jnp.where(lane == 1, mass, chosen)).T
     vst1[0] = packed[0:8]
@@ -435,7 +482,7 @@
         ),
     )(
         acc, stats, out_weight, residual, norm_gain[None, :], vocab_weight,
-        candidates[:, None], amateur[None, :],
+        candidates[None, :], amateur[None, :],
     )
     return hidden, contrast[0]
 

time: 177 us -> 140 us (0.79)
  Pallas kernels: 159 us -> 132 us
  local copies, waits for them, and re-layouts: 15.6 us -> 5.88 us
    pallas_call x1, Pallas kernels: 53.1 us -> 35.6 us  [attention(): pl.pallas_call(attention_kernel, grid_spec=pltpu.PrefetchScalarGridSpec(n...]
    unnamed x16 -> x2, local copies, waits for them, and re-layouts: 11.6 us -> 2.65 us
    pallas_call x1, Pallas kernels: 106 us -> 96.6 us  [tail(): pl.pallas_call(functools.partial(tail_kernel, seq, head, slots, nodes), i...]
where the time goes in v2:
time: 140 us
  Pallas kernels  132 us (94%)
  local copies, waits for them, and re-layouts  5.88 us (4%)
    pallas_call x1, Pallas kernels, tail(): pl.pallas_call(functools.partial(tail_kernel, seq, head, slots, nodes), i...  96.6 us
    pallas_call x1, Pallas kernels, attention(): pl.pallas_call(attention_kernel, grid_spec=pltpu.PrefetchScalarGridSpec(n...  35.6 us

profile of v2, /device:TPU:0, one launch (start us, length us, event | category | flops | bytes accessed | tf_op | source)
XLA Modules:
  0.0 140.1 jit_solution(9142897048878566119)
XLA Ops:
  0.6 0.7 subtract_clamp_fusion
  1.3 0.6 pad_add_fusion.meta_ref
  1.9 0.9 copy.15
  2.8 1.4 %broadcast_in_dim.17.gain_ref = bf16[1,16384]{1,0:T(2,128)(2,1)} reshape(bf16[16384]{0:T(1024)(128)(2,1)} %param.22) | data formatting | bytes 65536 | tf_op jit(solution)/shard_map/broadcast_in_dim | solution.py:484
  4.3 0.9 tile.10.tm_ref
  5.2 35.6 %shard_map.140 = (bf16[8,128,512]{2,1,0:T(8,128)(2,1)}, f32[8,8,512]{2,1,0:T(8,128)}) custom-call(s32[3]{0:T(128)} %pad_add_fusion.meta_ref, bf16[128,4096]{1,0:T(8,128)(2,1)} %q_ref.1, bf16[2,4096,256]{2,1,0:T(8,128)(2,1)} %k_ref.1, bf16[2,4096,256]{2,1,0:T(8,128)(2,1)} %v_ref.1, bf16[128,256]{1,0:T(8,128)(2,1)} %tk_ref.1, bf16[128,256]{1,0:T(8,128)(2,1)} %tv_ref.1, ...), custom_call_target="tpu_custom_call" | custom-call | flops 8589934592 | bytes 8388608 | tf_op jit(solution)/shard_map/pallas_call | solution.py:109
  40.8 96.6 %shard_map.141 = (bf16[128,512]{1,0:T(8,128)(2,1)}, f32[1,128]{1,0:T(1,128)}) custom-call(bf16[8,128,512]{2,1,0:T(8,128)(2,1)} %get-tuple-element.6.acc_hbm, f32[8,8,512]{2,1,0:T(8,128)} %get-tuple-element.7.st_hbm, bf16[4096,2048]{1,0:T(8,128)(2,1)} %wo_hbm.1, bf16[128,2048]{1,0:T(8,128)(2,1)} %res_ref.1, bf16[1,16384]{1,0:T(2,128)(2,1)} %broadcast_in_dim.17.gain_ref, ...), custom_call_target="tpu_custom_call" | custom-call | flops 10737418240 | bytes 83886080 | tf_op jit(solution)/shard_map/pallas_call | solution.py:448
  137.4 1.6 %copy.18 = bf16[128,512]{1,0:T(8,128)(2,1)} copy(bf16[128,512]{1,0:T(8,128)(2,1)} %get-tuple-element.12) | data formatting | bytes 262144
  139.0 1.1 copy.19
  (1 shorter events, 0.0 us)
